TPU v7x, 32 devices: a whole 2x2x4 slice. The times are simulated.
32 devices in a mesh: groups: 2 (over y), expert: 16 (over z, x, core), dp: 1.
Axes of the slice: x: 2, y: 2, z: 4, core: 2. Of those that a mesh axis runs over, the one named last changes fastest.
Arguments:
- tokens: bfloat16 [128, 3584], P(('groups', 'expert', 'dp')), parts along dimension 0, may hold values from -6 to 6
- cotangent: bfloat16 [128, 3584], P(('groups', 'expert', 'dp')), parts along dimension 0, may hold values from -6 to 6
- gate: bfloat16 [128, 8], P(('groups', 'expert', 'dp')), parts along dimension 0, may hold values from 0.019897461 to 0.5
- expert_ids: int32 [128, 8], P(('groups', 'expert', 'dp')), parts along dimension 0, may hold values from 0 to 15, all different within a row; in each aligned block of 4 rows (0 to 3, 4 to 7, ...) at most 4 rows name the same one
- w_in: bfloat16 [16, 3584, 1024], P('expert', None, 'dp'), may hold values from -0.09375 to 0.09375
- w_out: bfloat16 [16, 1024, 3584], P('expert', 'dp'), may hold values from -0.1875 to 0.1875
Outputs:
- tokens_grad: bfloat16 [128, 3584], P(('groups', 'expert', 'dp')), parts along dimension 0
- gate_grad: float32 [128, 8], P(('groups', 'expert', 'dp')), parts along dimension 0
- w_in_grad: bfloat16 [32, 3584, 1024], P(('groups', 'expert'), None, 'dp'), parts along dimension 0
- w_out_grad: bfloat16 [32, 1024, 3584], P(('groups', 'expert'), 'dp'), parts along dimension 0
There are 2 independent parts, one for each index of `groups`. A program takes and returns all parts, laid end to end along the dimension named above; an argument that names none is the same for every part. Nothing has to cross between parts.
Inputs may be any that keep to these rules, and one draw needn't show every extreme that they name: `expert_ids`: the 8 experts of a token differ. In each aligned block of 4 tokens (the tokens of one device), no expert is named by more than 4 tokens, a bound that some block reaches.
All inputs are finite; a program needn't handle non-finite values.
Results may differ from a plain program's by a relative error of at most 0.0064.
Values may be sent and summed in bfloat16 or wider, within the bound.
A program may use at most 128 MiB of HBM per device.

v0:
```python
import functools

import jax
import jax.numpy as jnp
from jax import lax
from jax.experimental import pallas as pl
from jax.experimental.pallas import tpu as pltpu
from jax.sharding import PartitionSpec as P

TOP = 8


def build_places(id_block, experts_all, capacity):
    tok_count = id_block.shape[0]
    routed = tok_count * TOP
    slots = experts_all * capacity
    flat_ids = id_block.reshape(routed)
    onehot = (flat_ids[:, None] == jnp.arange(experts_all, dtype=jnp.int32)[None, :]).astype(
        jnp.int32
    )
    ranks = jnp.cumsum(onehot, axis=0, dtype=jnp.int32) - 1
    position = jnp.sum(ranks * onehot, axis=1, dtype=jnp.int32)
    slot_index = flat_ids * capacity + position
    placing = jnp.arange(slots, dtype=jnp.int32)[:, None] == slot_index[None, :]
    place_rows = placing.astype(jnp.bfloat16)
    place_tokens = jnp.sum(placing.reshape(slots, tok_count, TOP).astype(jnp.int32), axis=2).astype(
        jnp.bfloat16
    )
    return (place_rows, place_tokens)


def shards(tokens, cotangent, gate, expert_ids, w_in, w_out):
    tok_count = tokens.shape[0]
    model_width = tokens.shape[1]
    local_experts = w_in.shape[0]
    expert_count = lax.axis_size("expert")
    data_count = lax.axis_size("dp")
    experts_all = local_experts * expert_count
    capacity = min(tok_count, max(2, 2 * tok_count * TOP // experts_all))
    routed = tok_count * TOP
    group_span = data_count * capacity
    group_ids = lax.all_gather(expert_ids, "dp", axis=0, tiled=True)

    def places_of(id_block):
        return build_places(id_block, experts_all, capacity)

    group_place_rows, group_place_tokens = jax.vmap(places_of)(
        group_ids.reshape(data_count, tok_count, TOP)
    )
    token_blocks = group_place_tokens.reshape(data_count, experts_all, capacity, tok_count)
    row_blocks = group_place_rows.reshape(data_count, experts_all, capacity, routed)
    all_tokens, all_cot, all_gate = (
        lax.all_gather(tokens, "dp", axis=0, tiled=True),
        lax.all_gather(cotangent, "dp", axis=0, tiled=True),
        lax.all_gather(gate, "dp", axis=0, tiled=True),
    )
    x_slots = jnp.einsum(
        "ject,jtd->ejcd",
        token_blocks,
        all_tokens.reshape(data_count, tok_count, model_width),
        preferred_element_type=jnp.float32,
    ).astype(jnp.bfloat16)
    dy_slots = jnp.einsum(
        "ject,jtd->ejcd",
        token_blocks,
        all_cot.reshape(data_count, tok_count, model_width),
        preferred_element_type=jnp.float32,
    ).astype(jnp.bfloat16)
    gate_slots = jnp.einsum(
        "jecr,jr->ejc",
        row_blocks,
        all_gate.reshape(data_count, routed),
        preferred_element_type=jnp.float32,
    ).astype(jnp.bfloat16)
    x_in, dy_in, g_in = (
        lax.all_to_all(x_slots, "expert", split_axis=0, concat_axis=0, tiled=True),
        lax.all_to_all(dy_slots, "expert", split_axis=0, concat_axis=0, tiled=True),
        lax.all_to_all(gate_slots, "expert", split_axis=0, concat_axis=0, tiled=True),
    )
    x_in = x_in.reshape(expert_count, local_experts, group_span, model_width)
    dy_in = dy_in.reshape(expert_count, local_experts, group_span, model_width)
    g_in = g_in.reshape(expert_count, local_experts, group_span)
    preact = jnp.einsum("slmd,ldh->slmh", x_in, w_in, preferred_element_type=jnp.float32)
    logistic = jax.nn.sigmoid(preact)
    hidden = (preact * logistic).astype(jnp.bfloat16)
    part_out = jnp.einsum("slmh,lhd->slmd", hidden, w_out, preferred_element_type=jnp.float32)
    score_part = jnp.sum(part_out * dy_in.astype(jnp.float32), axis=3).astype(jnp.bfloat16)
    dy_gated = (g_in.astype(jnp.float32)[..., None] * dy_in.astype(jnp.float32)).astype(
        jnp.bfloat16
    )
    hidden_grad = jnp.einsum("slmd,lhd->slmh", dy_gated, w_out, preferred_element_type=jnp.float32)
    preact_grad = (hidden_grad * logistic * (1.0 + preact * (1.0 - logistic))).astype(jnp.bfloat16)
    w_out_grad = jnp.einsum(
        "slmh,slmd->lhd", hidden, dy_gated, preferred_element_type=jnp.float32
    ).astype(jnp.bfloat16)
    w_in_grad = jnp.einsum(
        "slmd,slmh->ldh", x_in, preact_grad, preferred_element_type=jnp.float32
    ).astype(jnp.bfloat16)
    dx_part = jnp.einsum(
        "slmh,ldh->slmd", preact_grad, w_in, preferred_element_type=jnp.float32
    ).astype(jnp.bfloat16)
    back_rows, back_scores = (
        lax.all_to_all(dx_part, "expert", split_axis=0, concat_axis=0, tiled=True),
        lax.all_to_all(score_part, "expert", split_axis=0, concat_axis=0, tiled=True),
    )
    back_rows = back_rows.reshape(experts_all, data_count, capacity, model_width)
    back_scores = back_scores.reshape(experts_all, data_count, capacity)
    token_part = jnp.einsum(
        "ject,ejcd->jtd", token_blocks, back_rows, preferred_element_type=jnp.float32
    )
    gate_part = jnp.einsum(
        "jecr,ejc->jr", row_blocks, back_scores, preferred_element_type=jnp.float32
    )
    gate_part = gate_part.reshape(data_count, tok_count, TOP)
    token_total, gate_total = (
        lax.psum_scatter(token_part, "dp", scatter_dimension=0, tiled=True),
        lax.psum_scatter(gate_part, "dp", scatter_dimension=0, tiled=True),
    )
    tokens_grad = token_total.reshape(tok_count, model_width).astype(jnp.bfloat16)
    gate_grad = gate_total.reshape(tok_count, TOP)
    return (tokens_grad, gate_grad, w_in_grad, w_out_grad)


F32 = jnp.float32
BF16 = jnp.bfloat16
MESH = pl.DeviceIdType.MESH
VMEM_BYTES = 60 * 1024 * 1024
LANES = 128


def exchange_kernel(
    tok,
    cot,
    gate,
    ids,
    w_in_hbm,
    w_out_hbm,
    x_out,
    dyg_out,
    hid_out,
    dpre_out,
    sum_out,
    w_in,
    w_out,
    tb,
    cb,
    cmat,
    part,
    r1,
    s1,
    r2,
    acc,
    s2,
    r3,
    stage,
    w_sem,
    gather_send,
    gather_recv,
    r1_send,
    r1_recv,
    r2_send,
    r2_recv,
    r3_send,
    r3_recv,
):
    zs = tb.shape[2]
    quarter = tb.shape[4]
    half = part.shape[5]
    blocks = 4 * zs
    rows = 16 * blocks
    count = 4 * blocks
    hidden_units = w_in.shape[1]
    me = lax.axis_index("expert")
    c = lax.rem(me, 2)
    x = lax.rem(lax.div(me, 2), 2)
    z = lax.div(me, 4)

    def index(z_, x_, c_):
        return (z_ * 2 + x_) * 2 + c_

    sibling = index(z, x, 1 - c)
    across = index(z, 1 - x, c)

    weight_copies = [
        pltpu.make_async_copy(w_in_hbm, w_in, w_sem.at[0]),
        pltpu.make_async_copy(w_out_hbm, w_out, w_sem.at[1]),
    ]
    for copy in weight_copies:
        copy.start()

    barrier = pltpu.get_barrier_semaphore()
    peers = [sibling, across] + [index(lax.rem(z + d, zs), x, c) for d in range(1, zs)]
    for peer in peers:
        pl.semaphore_signal(barrier, inc=1, device_id={"expert": peer}, device_id_type=MESH)

    lane = lax.broadcasted_iota(jnp.int32, (4, LANES), 1)
    gates = jnp.zeros((4, LANES), F32)
    gate_f = gate[...].astype(F32)
    ids_v = ids[...]
    for k in range(TOP):
        gates = gates + jnp.where(lane == ids_v[:, k : k + 1], gate_f[:, k : k + 1], 0.0)
    for q in range(4):
        stage[4 * q : 4 * q + 4, 0:quarter] = tok[:, q * quarter : (q + 1) * quarter].astype(F32)
    tb[c, x, z] = stage[:, 0:quarter].astype(BF16)
    stage[:, quarter:] = jnp.zeros((16, LANES), F32)
    stage[0:4, quarter:] = gates
    for q in range(4):
        stage[4 * q : 4 * q + 4, 0:quarter] = cot[:, q * quarter : (q + 1) * quarter].astype(F32)
    cb[c, x, z] = stage[...].astype(BF16)

    pl.semaphore_wait(barrier, len(peers))

    bufs = (tb, cb)
    sent = []

    def remote(a, block, target, slot):
        return pltpu.make_async_remote_copy(
            src_ref=bufs[a].at[block],
            dst_ref=bufs[a].at[block],
            send_sem=gather_send.at[slot],
            recv_sem=gather_recv.at[(a,) + block],
            device_id={"expert": target},
            device_id_type=MESH,
        )

    def under(conds, action):
        if not conds:
            action()
            return
        cond = conds[0]
        for other in conds[1:]:
            cond = jnp.logical_and(cond, other)
        pl.when(cond)(action)

    def send(a, block, target, conds=()):
        slot = len(sent)
        under(conds, lambda: remote(a, block, target, slot).start())
        sent.append((a, block, target, conds))

    def arrive(a, block, conds=()):
        under(conds, lambda: remote(a, block, sibling, 0).wait_recv())

    has_up, has_down = z + 1 < zs, z >= 1
    up = index(jnp.minimum(z + 1, zs - 1), x, c)
    down = index(jnp.maximum(z - 1, 0), x, c)
    own = (c, x, z)
    send(0, own, across)
    send(1, own, up, (has_up,))
    send(1, own, down, (has_down,))
    send(0, own, up, (has_up,))
    send(0, own, down, (has_down,))
    send(1, own, across)
    send(0, own, sibling)
    send(1, own, sibling)
    beside = (c, 1 - x, z)
    arrive(0, beside)
    send(0, beside, up, (has_up,))
    send(0, beside, down, (has_down,))
    send(0, beside, sibling)
    for s in range(1, zs):
        below, above = jnp.maximum(z - s, 0), jnp.minimum(z + s, zs - 1)
        from_below, from_above = z - s >= 0, z + s < zs
        for a, x_ in ((1, x), (0, x), (0, 1 - x)):
            for zz, there, onward, target in (
                (below, from_below, has_up, up),
                (above, from_above, has_down, down),
            ):
                block = (c, x_, zz)
                arrive(a, block, (there,))
                if s < zs - 1:
                    send(a, block, target, (there, onward))
                if a == 1:
                    send(a, block, across, (there,))
                send(a, block, sibling, (there,))
    for d in range(zs):
        block = (c, 1 - x, lax.rem(z + d, zs))
        arrive(1, block)
        send(1, block, sibling)

    def order(shape, dim):
        r = lax.broadcasted_iota(jnp.int32, shape, dim)
        q = lax.div(r, count)
        b = lax.div(lax.rem(r, count), 4)
        return b * 16 + q * 4 + lax.rem(r, 4)

    shape = (rows, rows)
    to_rows = jnp.where(
        order(shape, 0) == lax.broadcasted_iota(jnp.int32, shape, 1), 1.0, 0.0
    ).astype(BF16)
    to_blocks = jnp.where(
        order(shape, 1) == lax.broadcasted_iota(jnp.int32, shape, 0), 1.0, 0.0
    ).astype(BF16)

    for a in range(2):
        for x_ in range(2):
            for zz in range(zs):
                arrive(a, (1 - c, x_, zz))

    x_rows = jnp.dot(to_rows, tb[...].reshape(rows, quarter), preferred_element_type=F32)
    c_rows = jnp.dot(to_rows, cb[...].reshape(rows, quarter + LANES), preferred_element_type=F32)
    lanes = lax.broadcasted_iota(jnp.int32, (count, LANES), 1)
    g = jnp.sum(jnp.where(lanes == me, c_rows[0:count, quarter:], 0.0), axis=1, keepdims=True)
    for q in range(4):
        columns = slice(q * quarter, (q + 1) * quarter)
        x_out[:, columns] = x_rows[q * count : (q + 1) * count].astype(BF16)
        c_q = c_rows[q * count : (q + 1) * count, 0:quarter]
        cmat[:, columns] = c_q.astype(BF16)
        dyg_out[:, columns] = (g * c_q).astype(BF16)

    for copy in weight_copies:
        copy.wait()

    tile = 256

    def hidden_tile(n, score):
        columns = pl.ds(pl.multiple_of(n * tile, tile), tile)
        pre = jnp.dot(x_out[...], w_in[:, columns], preferred_element_type=F32)
        back = lax.dot_general(
            cmat[...], w_out[columns, :], (((1,), (1,)), ((), ())), preferred_element_type=F32
        )
        logistic = jax.nn.sigmoid(pre)
        hidden = (pre * logistic).astype(BF16)
        hid_out[:, columns] = hidden
        dpre_out[:, columns] = (g * back * logistic * (1.0 + pre * (1.0 - logistic))).astype(BF16)
        return score + jnp.sum(hidden.astype(F32) * back, axis=1, keepdims=True)

    score = lax.fori_loop(0, hidden_units // tile, hidden_tile, jnp.zeros((count, 1), F32))
    score_lanes = jnp.where((lanes == me) & (g > 0.0), score, 0.0).astype(BF16)

    def r1_copy(h, x_):
        return pltpu.make_async_remote_copy(
            src_ref=part.at[h, 1 - c, x_],
            dst_ref=r1.at[h, x_],
            send_sem=r1_send.at[h, x_],
            recv_sem=r1_recv.at[h, x_],
            device_id={"expert": sibling},
            device_id_type=MESH,
        )

    def r2_copy(h):
        return pltpu.make_async_remote_copy(
            src_ref=s1.at[h],
            dst_ref=r2.at[h],
            send_sem=r2_send.at[h],
            recv_sem=r2_recv.at[h],
            device_id={"expert": across},
            device_id_type=MESH,
        )

    def r3_copy(h, d, slot):
        to = lax.rem(z + d, zs)
        return pltpu.make_async_remote_copy(
            src_ref=s2.at[h, to],
            dst_ref=r3.at[h, slot],
            send_sem=r3_send.at[h, to],
            recv_sem=r3_recv.at[h, slot],
            device_id={"expert": index(to, x, c)},
            device_id_type=MESH,
        )

    for h in range(2):
        width = half if h == 0 else quarter - half
        pieces = []
        for q in range(4):
            piece = lax.dot_general(
                dpre_out[...],
                w_in[q * quarter + h * half : q * quarter + h * half + width, :],
                (((1,), (1,)), ((), ())),
                preferred_element_type=F32,
            ).astype(BF16)
            if h == 1:
                extra = score_lanes if q == 0 else jnp.zeros((count, LANES), BF16)
                piece = jnp.concatenate([piece, extra], axis=1)
            pieces.append(piece)
        stacked = jnp.concatenate(pieces, axis=0)
        part[h] = (
            jnp.dot(to_blocks, stacked, preferred_element_type=F32)
            .astype(BF16)
            .reshape(2, 2, zs, 16, half)
        )
        r1_copy(h, 1 - x).start()
        r1_copy(h, x).start()

    for h in range(2):
        r1_copy(h, 1 - x).wait_recv()
        s1[h] = (part[h, c, 1 - x].astype(F32) + r1[h, 1 - x].astype(F32)).astype(BF16)
        r2_copy(h).start()
    for h in range(2):
        r1_copy(h, x).wait_recv()
        r2_copy(h).wait_recv()
        total = part[h, c, x].astype(F32) + r1[h, x].astype(F32) + r2[h].astype(F32)
        acc[h] = total
        s2[h] = total.astype(BF16)
        for d in range(1, zs):
            r3_copy(h, d, z).start()
    for h in range(2):
        final = acc[h, z]
        for d in range(1, zs):
            slot = lax.rem(z + d, zs)
            r3_copy(h, d, slot).wait_recv()
            final = final + r3[h, slot].astype(F32)
        sum_out[:, h * half : (h + 1) * half] = final

    for h in range(2):
        r1_copy(h, 0).wait_send()
        r1_copy(h, 1).wait_send()
        r2_copy(h).wait_send()
        for d in range(1, zs):
            r3_copy(h, d, z).wait_send()
    for slot, (a, block, target, conds) in enumerate(sent):
        under(
            conds,
            functools.partial(
                lambda a, block, target, slot: remote(a, block, target, slot).wait_send(),
                a, block, target, slot,
            ),
        )


def grads_kernel(x, dyg, hidden, dpre, sums, ids, tok_grad, gate_grad, w_in_grad, w_out_grad):
    over_rows = (((0,), (0,)), ((), ()))
    w_in_grad[...] = lax.dot_general(
        x[...], dpre[...], over_rows, preferred_element_type=F32
    ).astype(BF16)[None]
    w_out_grad[...] = lax.dot_general(
        hidden[...], dyg[...], over_rows, preferred_element_type=F32
    ).astype(BF16)[None]

    @pl.when(pl.program_id(0) == 0)
    def _():
        quarter = sums.shape[1] - LANES
        for q in range(4):
            tok_grad[:, q * quarter : (q + 1) * quarter] = sums[
                4 * q : 4 * q + 4, 0:quarter
            ].astype(BF16)
        scores = sums[0:4, quarter:]
        lane = lax.broadcasted_iota(jnp.int32, (4, LANES), 1)
        place = lax.broadcasted_iota(jnp.int32, (4, TOP), 1)
        ids_v = ids[...]
        result = jnp.zeros((4, TOP), F32)
        for k in range(TOP):
            value = jnp.sum(
                jnp.where(lane == ids_v[:, k : k + 1], scores, 0.0), axis=1, keepdims=True
            )
            result = jnp.where(place == k, value, result)
        gate_grad[...] = result


def fused_shards(tokens, cotangent, gate, expert_ids, w_in, w_out):
    tok_count, width = tokens.shape
    units = w_in.shape[2]
    zs = lax.axis_size("expert") // 4
    count = 4 * zs * tok_count
    quarter = width // 4
    half = (quarter + LANES) // 2
    vmem = pl.BlockSpec(memory_space=pltpu.VMEM)
    hbm = pl.BlockSpec(memory_space=pl.ANY)
    sends = 10 + 1 + (zs - 1) * 18 + zs
    dma = pltpu.SemaphoreType.DMA
    weight = width * units
    x, dyg, hidden, dpre, sums = pl.pallas_call(
        exchange_kernel,
        out_shape=(
            jax.ShapeDtypeStruct((count, width), BF16),
            jax.ShapeDtypeStruct((count, width), BF16),
            jax.ShapeDtypeStruct((count, units), BF16),
            jax.ShapeDtypeStruct((count, units), BF16),
            jax.ShapeDtypeStruct((16, quarter + LANES), F32),
        ),
        in_specs=[vmem, vmem, vmem, vmem, hbm, hbm],
        out_specs=[vmem] * 5,
        scratch_shapes=[
            pltpu.VMEM((width, units), BF16),
            pltpu.VMEM((units, width), BF16),
            pltpu.VMEM((2, 2, zs, 16, quarter), BF16),
            pltpu.VMEM((2, 2, zs, 16, quarter + LANES), BF16),
            pltpu.VMEM((count, width), BF16),
            pltpu.VMEM((2, 2, 2, zs, 16, half), BF16),
            pltpu.VMEM((2, 2, zs, 16, half), BF16),
            pltpu.VMEM((2, zs, 16, half), BF16),
            pltpu.VMEM((2, zs, 16, half), BF16),
            pltpu.VMEM((2, zs, 16, half), F32),
            pltpu.VMEM((2, zs, 16, half), BF16),
            pltpu.VMEM((2, zs, 16, half), BF16),
            pltpu.VMEM((16, quarter + LANES), F32),
            dma((2,)),
            dma((sends,)),
            dma((2, 2, 2, zs)),
            dma((2, 2)),
            dma((2, 2)),
            dma((2,)),
            dma((2,)),
            dma((2, zs)),
            dma((2, zs)),
        ],
        compiler_params=pltpu.CompilerParams(
            collective_id=0, has_side_effects=True, vmem_limit_bytes=VMEM_BYTES
        ),
        cost_estimate=pl.CostEstimate(
            flops=6 * count * weight, bytes_accessed=4 * weight, transcendentals=count * units
        ),
    )(tokens, cotangent, gate, expert_ids, w_in[0], w_out[0])

    steps = 7
    wide = width // steps
    return pl.pallas_call(
        grads_kernel,
        grid=(steps,),
        out_shape=(
            jax.ShapeDtypeStruct((tok_count, width), BF16),
            jax.ShapeDtypeStruct((tok_count, TOP), F32),
            jax.ShapeDtypeStruct((1, width, units), BF16),
            jax.ShapeDtypeStruct((1, units, width), BF16),
        ),
        in_specs=[
            pl.BlockSpec((count, wide), lambda i: (0, i)),
            pl.BlockSpec((count, wide), lambda i: (0, i)),
            pl.BlockSpec((count, units), lambda i: (0, 0)),
            pl.BlockSpec((count, units), lambda i: (0, 0)),
            pl.BlockSpec((16, quarter + LANES), lambda i: (0, 0)),
            pl.BlockSpec((tok_count, TOP), lambda i: (0, 0)),
        ],
        out_specs=(
            pl.BlockSpec((tok_count, width), lambda i: (0, 0)),
            pl.BlockSpec((tok_count, TOP), lambda i: (0, 0)),
            pl.BlockSpec((1, wide, units), lambda i: (0, i, 0)),
            pl.BlockSpec((1, units, wide), lambda i: (0, 0, i)),
        ),
        compiler_params=pltpu.CompilerParams(vmem_limit_bytes=VMEM_BYTES),
        cost_estimate=pl.CostEstimate(
            flops=4 * count * weight, bytes_accessed=4 * weight, transcendentals=0
        ),
    )(x, dyg, hidden, dpre, sums, expert_ids)


def solution(mesh):
    fused = mesh.shape["dp"] == 1 and mesh.shape["expert"] == 16
    return jax.shard_map(
        fused_shards if fused else shards,
        mesh=mesh,
        in_specs=(
            P(("groups", "expert", "dp"), None),
            P(("groups", "expert", "dp"), None),
            P(("groups", "expert", "dp"), None),
            P(("groups", "expert", "dp"), None),
            P("expert", None, "dp"),
            P("expert", "dp", None),
        ),
        out_specs=(
            P(("groups", "expert", "dp"), None),
            P(("groups", "expert", "dp"), None),
            P(("groups", "expert"), None, "dp"),
            P(("groups", "expert"), "dp", None),
        ),
        check_vma=False,
    )
```

profile of v0, /device:TPU:0, one launch (start us, length us, event | category | flops | bytes accessed | tf_op | source)
XLA Modules:
  0.0 47.8 jit_solution(17615653424908469929)
XLA Ops:
  0.6 37.8 %shard_map.93 = (bf16[64,3584]{1,0:T(8,128)(2,1)}, bf16[64,3584]{1,0:T(8,128)(2,1)}, bf16[64,1024]{1,0:T(8,128)(2,1)}, bf16[64,1024]{1,0:T(8,128)(2,1)}, f32[16,1024]{1,0:T(8,128)}) custom-call(bf16[4,3584]{1,0:T(4,128)(2,1)} %tok.1, bf16[4,3584]{1,0:T(4,128)(2,1)} %cot.1, bf16[4,8]{1,0:T(4,128)(2,1)} %gate.1, s32[4,8]{1,0:T(4,128)} %ids.3, ...), custom_call_target="tpu_custom_call" | custom-call | flops 1409286144 | bytes 14680064 | tf_op jit(solution)/shard_map/pallas_call | solution.py:461
  38.4 9.4 %shard_map.94 = (bf16[4,3584]{1,0:T(4,128)(2,1)}, f32[4,8]{1,0:T(4,128)}, bf16[1,3584,1024]{2,1,0:T(8,128)(2,1)}, bf16[1,1024,3584]{2,1,0:T(8,128)(2,1)}) custom-call(bf16[64,3584]{1,0:T(8,128)(2,1)} %get-tuple-element.9.x, bf16[64,3584]{1,0:T(8,128)(2,1)} %get-tuple-element.10.dyg, bf16[64,1024]{1,0:T(8,128)(2,1)} %get-tuple-element.11.hidden, ...), custom_call_target="tpu_custom_call" | custom-call | flops 939524096 | bytes 14680064 | tf_op jit(solution)/shard_map/pallas_call | solution.py:506
where the time goes:
time: 48.2 us; the launch traced here: 47.8 us
  Pallas kernels  47.1 us (98%)
  between operations  0.64 us (1%)
    pallas_call x1, Pallas kernels, fused_shards(): pl.pallas_call(exchange_kernel, out_shape=(jax.ShapeDtypeStruct((count, w...  37.8 us
    pallas_call x1, Pallas kernels, fused_shards(): pl.pallas_call(grads_kernel, grid=(steps,), out_shape=(jax.ShapeDtypeStru...  9.37 us

commit v1 on v0

--- a/solution.py
+++ b/solution.py
@@ -124,7 +124,8 @@
 F32 = jnp.float32
 BF16 = jnp.bfloat16
 MESH = pl.DeviceIdType.MESH
-VMEM_BYTES = 60 * 1024 * 1024
+VMEM_BYTES = 58 * 1024 * 1024
+CHUNKS = 4
 LANES = 128
 
 
@@ -153,6 +154,9 @@
     s2,
     r3,
     stage,
+    to_rows,
+    to_blocks,
+    pre_s,
     w_sem,
     gather_send,
     gather_recv,
@@ -240,91 +244,83 @@
     def arrive(a, block, conds=()):
         under(conds, lambda: remote(a, block, sibling, 0).wait_recv())
 
-    has_up, has_down = z + 1 < zs, z >= 1
-    up = index(jnp.minimum(z + 1, zs - 1), x, c)
-    down = index(jnp.maximum(z - 1, 0), x, c)
     own = (c, x, z)
-    send(0, own, across)
-    send(1, own, up, (has_up,))
-    send(1, own, down, (has_down,))
-    send(0, own, up, (has_up,))
-    send(0, own, down, (has_down,))
-    send(1, own, across)
+    for a in range(2):
+        for d in range(1, zs):
+            zz = lax.rem(z + d, zs)
+            send(a, own, index(zz, x, c))
+        send(a, own, across)
     send(0, own, sibling)
     send(1, own, sibling)
-    beside = (c, 1 - x, z)
-    arrive(0, beside)
-    send(0, beside, up, (has_up,))
-    send(0, beside, down, (has_down,))
-    send(0, beside, sibling)
-    for s in range(1, zs):
-        below, above = jnp.maximum(z - s, 0), jnp.minimum(z + s, zs - 1)
-        from_below, from_above = z - s >= 0, z + s < zs
-        for a, x_ in ((1, x), (0, x), (0, 1 - x)):
-            for zz, there, onward, target in (
-                (below, from_below, has_up, up),
-                (above, from_above, has_down, down),
-            ):
-                block = (c, x_, zz)
-                arrive(a, block, (there,))
-                if s < zs - 1:
-                    send(a, block, target, (there, onward))
-                if a == 1:
-                    send(a, block, across, (there,))
-                send(a, block, sibling, (there,))
+
+    low, mid = 4, count.bit_length() - 1
+
+    def order(shape, dim):
+        r = lax.broadcasted_iota(jnp.int32, shape, dim)
+        q = lax.shift_right_logical(r, mid)
+        b = lax.shift_right_logical(r & (count - 1), 2)
+        return lax.shift_left(b, low) + lax.shift_left(q, 2) + (r & 3)
+
+    shape = (rows, rows)
+    to_rows[...] = jnp.where(
+        order(shape, 0) == lax.broadcasted_iota(jnp.int32, shape, 1), 1.0, 0.0
+    ).astype(BF16)
+    to_blocks[...] = jnp.where(
+        order(shape, 1) == lax.broadcasted_iota(jnp.int32, shape, 0), 1.0, 0.0
+    ).astype(BF16)
+
+    for a in range(2):
+        for d in range(1, zs):
+            block = (c, x, lax.rem(z + d, zs))
+            arrive(a, block)
+            send(a, block, across)
+            send(a, block, sibling)
     for d in range(zs):
         block = (c, 1 - x, lax.rem(z + d, zs))
+        arrive(0, block)
+        send(0, block, sibling)
+
+    for x_ in range(2):
+        for zz in range(zs):
+            arrive(0, (1 - c, x_, zz))
+    x_rows = jnp.dot(to_rows[...], tb[...].reshape(rows, quarter), preferred_element_type=F32)
+    for q in range(4):
+        x_out[:, q * quarter : (q + 1) * quarter] = x_rows[q * count : (q + 1) * count].astype(BF16)
+
+    weight_copies[0].wait()
+    tile = hidden_units // zs
+    for n in range(zs):
+        columns = slice(n * tile, (n + 1) * tile)
+        pre_s[:, columns] = jnp.dot(x_out[...], w_in[:, columns], preferred_element_type=F32)
+        block = (c, 1 - x, lax.rem(z + n, zs))
         arrive(1, block)
         send(1, block, sibling)
 
-    def order(shape, dim):
-        r = lax.broadcasted_iota(jnp.int32, shape, dim)
-        q = lax.div(r, count)
-        b = lax.div(lax.rem(r, count), 4)
-        return b * 16 + q * 4 + lax.rem(r, 4)
-
-    shape = (rows, rows)
-    to_rows = jnp.where(
-        order(shape, 0) == lax.broadcasted_iota(jnp.int32, shape, 1), 1.0, 0.0
-    ).astype(BF16)
-    to_blocks = jnp.where(
-        order(shape, 1) == lax.broadcasted_iota(jnp.int32, shape, 0), 1.0, 0.0
-    ).astype(BF16)
-
-    for a in range(2):
-        for x_ in range(2):
-            for zz in range(zs):
-                arrive(a, (1 - c, x_, zz))
-
-    x_rows = jnp.dot(to_rows, tb[...].reshape(rows, quarter), preferred_element_type=F32)
-    c_rows = jnp.dot(to_rows, cb[...].reshape(rows, quarter + LANES), preferred_element_type=F32)
+    for x_ in range(2):
+        for zz in range(zs):
+            arrive(1, (1 - c, x_, zz))
+    c_rows = jnp.dot(to_rows[...], cb[...].reshape(rows, quarter + LANES), preferred_element_type=F32)
     lanes = lax.broadcasted_iota(jnp.int32, (count, LANES), 1)
     g = jnp.sum(jnp.where(lanes == me, c_rows[0:count, quarter:], 0.0), axis=1, keepdims=True)
     for q in range(4):
         columns = slice(q * quarter, (q + 1) * quarter)
-        x_out[:, columns] = x_rows[q * count : (q + 1) * count].astype(BF16)
         c_q = c_rows[q * count : (q + 1) * count, 0:quarter]
         cmat[:, columns] = c_q.astype(BF16)
         dyg_out[:, columns] = (g * c_q).astype(BF16)
 
-    for copy in weight_copies:
-        copy.wait()
-
-    tile = 256
-
-    def hidden_tile(n, score):
-        columns = pl.ds(pl.multiple_of(n * tile, tile), tile)
-        pre = jnp.dot(x_out[...], w_in[:, columns], preferred_element_type=F32)
+    weight_copies[1].wait()
+    score = jnp.zeros((count, 1), F32)
+    for n in range(zs):
+        columns = slice(n * tile, (n + 1) * tile)
         back = lax.dot_general(
             cmat[...], w_out[columns, :], (((1,), (1,)), ((), ())), preferred_element_type=F32
         )
+        pre = pre_s[:, columns]
         logistic = jax.nn.sigmoid(pre)
         hidden = (pre * logistic).astype(BF16)
         hid_out[:, columns] = hidden
         dpre_out[:, columns] = (g * back * logistic * (1.0 + pre * (1.0 - logistic))).astype(BF16)
-        return score + jnp.sum(hidden.astype(F32) * back, axis=1, keepdims=True)
-
-    score = lax.fori_loop(0, hidden_units // tile, hidden_tile, jnp.zeros((count, 1), F32))
+        score = score + jnp.sum(hidden.astype(F32) * back, axis=1, keepdims=True)
     score_lanes = jnp.where((lanes == me) & (g > 0.0), score, 0.0).astype(BF16)
 
     def r1_copy(h, x_):
@@ -358,8 +354,8 @@
             device_id_type=MESH,
         )
 
-    for h in range(2):
-        width = half if h == 0 else quarter - half
+    def row_grads(h):
+        width = half if h < CHUNKS - 1 else half - LANES
         pieces = []
         for q in range(4):
             piece = lax.dot_general(
@@ -368,24 +364,25 @@
                 (((1,), (1,)), ((), ())),
                 preferred_element_type=F32,
             ).astype(BF16)
-            if h == 1:
+            if width < half:
                 extra = score_lanes if q == 0 else jnp.zeros((count, LANES), BF16)
                 piece = jnp.concatenate([piece, extra], axis=1)
             pieces.append(piece)
         stacked = jnp.concatenate(pieces, axis=0)
         part[h] = (
-            jnp.dot(to_blocks, stacked, preferred_element_type=F32)
+            jnp.dot(to_blocks[...], stacked, preferred_element_type=F32)
             .astype(BF16)
             .reshape(2, 2, zs, 16, half)
         )
         r1_copy(h, 1 - x).start()
         r1_copy(h, x).start()
 
-    for h in range(2):
+    def add_cores(h):
         r1_copy(h, 1 - x).wait_recv()
         s1[h] = (part[h, c, 1 - x].astype(F32) + r1[h, 1 - x].astype(F32)).astype(BF16)
         r2_copy(h).start()
-    for h in range(2):
+
+    def add_across(h):
         r1_copy(h, x).wait_recv()
         r2_copy(h).wait_recv()
         total = part[h, c, x].astype(F32) + r1[h, x].astype(F32) + r2[h].astype(F32)
@@ -393,7 +390,20 @@
         s2[h] = total.astype(BF16)
         for d in range(1, zs):
             r3_copy(h, d, z).start()
-    for h in range(2):
+
+    row_grads(0)
+    row_grads(1)
+    add_cores(0)
+    row_grads(2)
+    add_cores(1)
+    row_grads(3)
+    add_cores(2)
+    add_across(0)
+    add_cores(3)
+    add_across(1)
+    add_across(2)
+    add_across(3)
+    for h in range(CHUNKS):
         final = acc[h, z]
         for d in range(1, zs):
             slot = lax.rem(z + d, zs)
@@ -401,7 +411,7 @@
             final = final + r3[h, slot].astype(F32)
         sum_out[:, h * half : (h + 1) * half] = final
 
-    for h in range(2):
+    for h in range(CHUNKS):
         r1_copy(h, 0).wait_send()
         r1_copy(h, 1).wait_send()
         r2_copy(h).wait_send()
@@ -417,33 +427,51 @@
         )
 
 
-def grads_kernel(x, dyg, hidden, dpre, sums, ids, tok_grad, gate_grad, w_in_grad, w_out_grad):
-    over_rows = (((0,), (0,)), ((), ()))
-    w_in_grad[...] = lax.dot_general(
-        x[...], dpre[...], over_rows, preferred_element_type=F32
-    ).astype(BF16)[None]
-    w_out_grad[...] = lax.dot_general(
-        hidden[...], dyg[...], over_rows, preferred_element_type=F32
-    ).astype(BF16)[None]
-
-    @pl.when(pl.program_id(0) == 0)
-    def _():
-        quarter = sums.shape[1] - LANES
-        for q in range(4):
-            tok_grad[:, q * quarter : (q + 1) * quarter] = sums[
-                4 * q : 4 * q + 4, 0:quarter
-            ].astype(BF16)
-        scores = sums[0:4, quarter:]
-        lane = lax.broadcasted_iota(jnp.int32, (4, LANES), 1)
-        place = lax.broadcasted_iota(jnp.int32, (4, TOP), 1)
-        ids_v = ids[...]
-        result = jnp.zeros((4, TOP), F32)
-        for k in range(TOP):
-            value = jnp.sum(
-                jnp.where(lane == ids_v[:, k : k + 1], scores, 0.0), axis=1, keepdims=True
-            )
-            result = jnp.where(place == k, value, result)
-        gate_grad[...] = result
+def grads_kernel(
+    x, dyg, hidden, dpre, sums, ids, tok_grad, gate_grad, w_in_grad, w_out_grad,
+    x_t, hidden_t, in_buf, out_buf, in_sem, out_sem,
+):
+    in_parts, in_rows = in_sem.shape[0], in_buf.shape[0] // in_sem.shape[0]
+    out_parts, out_rows = out_sem.shape[0], out_buf.shape[0] // out_sem.shape[0]
+
+    def in_copy(n, rows):
+        return pltpu.make_async_copy(in_buf.at[rows], w_in_grad.at[0, rows], in_sem.at[n])
+
+    def out_copy(n, rows):
+        return pltpu.make_async_copy(out_buf.at[rows], w_out_grad.at[0, rows], out_sem.at[n])
+
+    for n in range(out_parts):
+        rows = pl.ds(n * out_rows, out_rows)
+        hidden_t[rows, :] = hidden[:, n * out_rows : (n + 1) * out_rows].T
+        out_buf[rows, :] = jnp.dot(
+            hidden_t[rows, :], dyg[...], preferred_element_type=F32
+        ).astype(BF16)
+        out_copy(n, rows).start()
+    for n in range(in_parts):
+        rows = pl.ds(n * in_rows, in_rows)
+        x_t[rows, :] = x[:, n * in_rows : (n + 1) * in_rows].T
+        in_buf[rows, :] = jnp.dot(
+            x_t[rows, :], dpre[...], preferred_element_type=F32
+        ).astype(BF16)
+        in_copy(n, rows).start()
+
+    quarter = sums.shape[1] - LANES
+    for q in range(4):
+        tok_grad[:, q * quarter : (q + 1) * quarter] = sums[4 * q : 4 * q + 4, 0:quarter].astype(BF16)
+    scores = sums[0:4, quarter:]
+    lane = lax.broadcasted_iota(jnp.int32, (4, LANES), 1)
+    place = lax.broadcasted_iota(jnp.int32, (4, TOP), 1)
+    ids_v = ids[...]
+    result = jnp.zeros((4, TOP), F32)
+    for k in range(TOP):
+        value = jnp.sum(jnp.where(lane == ids_v[:, k : k + 1], scores, 0.0), axis=1, keepdims=True)
+        result = jnp.where(place == k, value, result)
+    gate_grad[...] = result
+
+    for n in range(out_parts):
+        out_copy(n, pl.ds(n * out_rows, out_rows)).wait()
+    for n in range(in_parts):
+        in_copy(n, pl.ds(n * in_rows, in_rows)).wait()
 
 
 def fused_shards(tokens, cotangent, gate, expert_ids, w_in, w_out):
@@ -452,9 +480,9 @@
     zs = lax.axis_size("expert") // 4
     count = 4 * zs * tok_count
     quarter = width // 4
-    half = (quarter + LANES) // 2
+    half = (quarter + LANES) // CHUNKS
     vmem = pl.BlockSpec(memory_space=pltpu.VMEM)
-    hbm = pl.BlockSpec(memory_space=pl.ANY)
+    hbm = pl.BlockSpec(memory_space=pltpu.HBM)
     sends = 10 + 1 + (zs - 1) * 18 + zs
     dma = pltpu.SemaphoreType.DMA
     weight = width * units
@@ -475,23 +503,26 @@
             pltpu.VMEM((2, 2, zs, 16, quarter), BF16),
             pltpu.VMEM((2, 2, zs, 16, quarter + LANES), BF16),
             pltpu.VMEM((count, width), BF16),
-            pltpu.VMEM((2, 2, 2, zs, 16, half), BF16),
-            pltpu.VMEM((2, 2, zs, 16, half), BF16),
-            pltpu.VMEM((2, zs, 16, half), BF16),
-            pltpu.VMEM((2, zs, 16, half), BF16),
-            pltpu.VMEM((2, zs, 16, half), F32),
-            pltpu.VMEM((2, zs, 16, half), BF16),
-            pltpu.VMEM((2, zs, 16, half), BF16),
+            pltpu.VMEM((CHUNKS, 2, 2, zs, 16, half), BF16),
+            pltpu.VMEM((CHUNKS, 2, zs, 16, half), BF16),
+            pltpu.VMEM((CHUNKS, zs, 16, half), BF16),
+            pltpu.VMEM((CHUNKS, zs, 16, half), BF16),
+            pltpu.VMEM((CHUNKS, zs, 16, half), F32),
+            pltpu.VMEM((CHUNKS, zs, 16, half), BF16),
+            pltpu.VMEM((CHUNKS, zs, 16, half), BF16),
             pltpu.VMEM((16, quarter + LANES), F32),
+            pltpu.VMEM((4 * count, 4 * count), BF16),
+            pltpu.VMEM((4 * count, 4 * count), BF16),
+            pltpu.VMEM((count, units), F32),
             dma((2,)),
             dma((sends,)),
             dma((2, 2, 2, zs)),
-            dma((2, 2)),
-            dma((2, 2)),
-            dma((2,)),
-            dma((2,)),
-            dma((2, zs)),
-            dma((2, zs)),
+            dma((CHUNKS, 2)),
+            dma((CHUNKS, 2)),
+            dma((CHUNKS,)),
+            dma((CHUNKS,)),
+            dma((CHUNKS, zs)),
+            dma((CHUNKS, zs)),
         ],
         compiler_params=pltpu.CompilerParams(
             collective_id=0, has_side_effects=True, vmem_limit_bytes=VMEM_BYTES
@@ -501,31 +532,24 @@
         ),
     )(tokens, cotangent, gate, expert_ids, w_in[0], w_out[0])
 
-    steps = 7
-    wide = width // steps
     return pl.pallas_call(
         grads_kernel,
-        grid=(steps,),
         out_shape=(
             jax.ShapeDtypeStruct((tok_count, width), BF16),
             jax.ShapeDtypeStruct((tok_count, TOP), F32),
             jax.ShapeDtypeStruct((1, width, units), BF16),
             jax.ShapeDtypeStruct((1, units, width), BF16),
         ),
-        in_specs=[
-            pl.BlockSpec((count, wide), lambda i: (0, i)),
-            pl.BlockSpec((count, wide), lambda i: (0, i)),
-            pl.BlockSpec((count, units), lambda i: (0, 0)),
-            pl.BlockSpec((count, units), lambda i: (0, 0)),
-            pl.BlockSpec((16, quarter + LANES), lambda i: (0, 0)),
-            pl.BlockSpec((tok_count, TOP), lambda i: (0, 0)),
+        in_specs=[vmem] * 6,
+        out_specs=(vmem, vmem, hbm, hbm),
+        scratch_shapes=[
+            pltpu.VMEM((width, count), BF16),
+            pltpu.VMEM((units, count), BF16),
+            pltpu.VMEM((width, units), BF16),
+            pltpu.VMEM((units, width), BF16),
+            dma((14,)),
+            dma((8,)),
         ],
-        out_specs=(
-            pl.BlockSpec((tok_count, width), lambda i: (0, 0)),
-            pl.BlockSpec((tok_count, TOP), lambda i: (0, 0)),
-            pl.BlockSpec((1, wide, units), lambda i: (0, i, 0)),
-            pl.BlockSpec((1, units, wide), lambda i: (0, 0, i)),
-        ),
         compiler_params=pltpu.CompilerParams(vmem_limit_bytes=VMEM_BYTES),
         cost_estimate=pl.CostEstimate(
             flops=4 * count * weight, bytes_accessed=4 * weight, transcendentals=0

time: 48.2 us -> 45.1 us (0.936)
  Pallas kernels: 47.1 us -> 44.3 us
    pallas_call x1, Pallas kernels: 9.37 us -> 7.67 us  [fused_shards(): pl.pallas_call(grads_kernel, out_shape=(jax.ShapeDtypeStruct((tok_count,...]
    pallas_call x1, Pallas kernels: 37.8 us -> 36.6 us  [fused_shards(): pl.pallas_call(exchange_kernel, out_shape=(jax.ShapeDtypeStruct((count, w...]
where the time goes in v1:
time: 45.1 us; the launch traced here: 44.9 us
  Pallas kernels  44.3 us (98%)
  between operations  0.64 us (1%)
    pallas_call x1, Pallas kernels, fused_shards(): pl.pallas_call(exchange_kernel, out_shape=(jax.ShapeDtypeStruct((count, w...  36.6 us
    pallas_call x1, Pallas kernels, fused_shards(): pl.pallas_call(grads_kernel, out_shape=(jax.ShapeDtypeStruct((tok_count,...  7.67 us

profile of v1, /device:TPU:0, one launch (start us, length us, event | category | flops | bytes accessed | tf_op | source)
XLA Modules:
  0.0 44.9 jit_solution(14681528536406052021)
XLA Ops:
  0.6 36.6 %shard_map.93 = (bf16[64,3584]{1,0:T(8,128)(2,1)}, bf16[64,3584]{1,0:T(8,128)(2,1)}, bf16[64,1024]{1,0:T(8,128)(2,1)}, bf16[64,1024]{1,0:T(8,128)(2,1)}, f32[16,1024]{1,0:T(8,128)}) custom-call(bf16[4,3584]{1,0:T(4,128)(2,1)} %tok.1, bf16[4,3584]{1,0:T(4,128)(2,1)} %cot.1, bf16[4,8]{1,0:T(4,128)(2,1)} %gate.1, s32[4,8]{1,0:T(4,128)} %ids.3, ...), custom_call_target="tpu_custom_call" | custom-call | flops 1409286144 | bytes 14680064 | tf_op jit(solution)/shard_map/pallas_call | solution.py:489
  37.3 7.7 %shard_map.94 = (bf16[4,3584]{1,0:T(4,128)(2,1)}, f32[4,8]{1,0:T(4,128)}, bf16[1,3584,1024]{2,1,0:T(8,128)(2,1)}, bf16[1,1024,3584]{2,1,0:T(8,128)(2,1)}) custom-call(bf16[64,3584]{1,0:T(8,128)(2,1)} %get-tuple-element.9.x, bf16[64,3584]{1,0:T(8,128)(2,1)} %get-tuple-element.10.dyg, bf16[64,1024]{1,0:T(8,128)(2,1)} %get-tuple-element.11.hidden, ...), custom_call_target="tpu_custom_call" | custom-call | flops 939524096 | bytes 14680064 | tf_op jit(solution)/shard_map/pallas_call | solution.py:535

commit v2 on v1

--- a/solution.py
+++ b/solution.py
@@ -218,11 +218,12 @@
     sent = []
 
     def remote(a, block, target, slot):
+        sem = block if len(block) == 3 else block + (0,)
         return pltpu.make_async_remote_copy(
             src_ref=bufs[a].at[block],
             dst_ref=bufs[a].at[block],
             send_sem=gather_send.at[slot],
-            recv_sem=gather_recv.at[(a,) + block],
+            recv_sem=gather_recv.at[(a,) + sem],
             device_id={"expert": target},
             device_id_type=MESH,
         )
@@ -246,12 +247,10 @@
 
     own = (c, x, z)
     for a in range(2):
-        for d in range(1, zs):
+        for d in (2, 3, 1) if zs == 4 else range(1, zs):
             zz = lax.rem(z + d, zs)
             send(a, own, index(zz, x, c))
         send(a, own, across)
-    send(0, own, sibling)
-    send(1, own, sibling)
 
     low, mid = 4, count.bit_length() - 1
 
@@ -274,15 +273,13 @@
             block = (c, x, lax.rem(z + d, zs))
             arrive(a, block)
             send(a, block, across)
-            send(a, block, sibling)
+        send(a, (c, x), sibling)
     for d in range(zs):
-        block = (c, 1 - x, lax.rem(z + d, zs))
-        arrive(0, block)
-        send(0, block, sibling)
+        arrive(0, (c, 1 - x, lax.rem(z + d, zs)))
+    send(0, (c, 1 - x), sibling)
 
     for x_ in range(2):
-        for zz in range(zs):
-            arrive(0, (1 - c, x_, zz))
+        arrive(0, (1 - c, x_))
     x_rows = jnp.dot(to_rows[...], tb[...].reshape(rows, quarter), preferred_element_type=F32)
     for q in range(4):
         x_out[:, q * quarter : (q + 1) * quarter] = x_rows[q * count : (q + 1) * count].astype(BF16)
@@ -292,13 +289,11 @@
     for n in range(zs):
         columns = slice(n * tile, (n + 1) * tile)
         pre_s[:, columns] = jnp.dot(x_out[...], w_in[:, columns], preferred_element_type=F32)
-        block = (c, 1 - x, lax.rem(z + n, zs))
-        arrive(1, block)
-        send(1, block, sibling)
+        arrive(1, (c, 1 - x, lax.rem(z + n, zs)))
+    send(1, (c, 1 - x), sibling)
 
     for x_ in range(2):
-        for zz in range(zs):
-            arrive(1, (1 - c, x_, zz))
+        arrive(1, (1 - c, x_))
     c_rows = jnp.dot(to_rows[...], cb[...].reshape(rows, quarter + LANES), preferred_element_type=F32)
     lanes = lax.broadcasted_iota(jnp.int32, (count, LANES), 1)
     g = jnp.sum(jnp.where(lanes == me, c_rows[0:count, quarter:], 0.0), axis=1, keepdims=True)
@@ -388,7 +383,7 @@
         total = part[h, c, x].astype(F32) + r1[h, x].astype(F32) + r2[h].astype(F32)
         acc[h] = total
         s2[h] = total.astype(BF16)
-        for d in range(1, zs):
+        for d in (2, 3, 1) if zs == 4 else range(1, zs):
             r3_copy(h, d, z).start()
 
     row_grads(0)

time: 45.1 us -> 44.8 us (level)
  no operation moved by 1% of the time
where the time goes in v2:
time: 44.8 us; the launch traced here: 44.6 us
  Pallas kernels  44 us (98%)
  between operations  0.64 us (1%)
    pallas_call x1, Pallas kernels, fused_shards(): pl.pallas_call(exchange_kernel, out_shape=(jax.ShapeDtypeStruct((count, w...  36.3 us
    pallas_call x1, Pallas kernels, fused_shards(): pl.pallas_call(grads_kernel, out_shape=(jax.ShapeDtypeStruct((tok_count,...  7.67 us

profile of v2, /device:TPU:0, one launch (start us, length us, event | category | flops | bytes accessed | tf_op | source)
XLA Modules:
  0.0 44.6 jit_solution(4260194610802811856)
XLA Ops:
  0.6 36.3 %shard_map.93 = (bf16[64,3584]{1,0:T(8,128)(2,1)}, bf16[64,3584]{1,0:T(8,128)(2,1)}, bf16[64,1024]{1,0:T(8,128)(2,1)}, bf16[64,1024]{1,0:T(8,128)(2,1)}, f32[16,1024]{1,0:T(8,128)}) custom-call(bf16[4,3584]{1,0:T(4,128)(2,1)} %tok.1, bf16[4,3584]{1,0:T(4,128)(2,1)} %cot.1, bf16[4,8]{1,0:T(4,128)(2,1)} %gate.1, s32[4,8]{1,0:T(4,128)} %ids.3, ...), custom_call_target="tpu_custom_call" | custom-call | flops 1409286144 | bytes 14680064 | tf_op jit(solution)/shard_map/pallas_call | solution.py:484
  37.0 7.7 %shard_map.94 = (bf16[4,3584]{1,0:T(4,128)(2,1)}, f32[4,8]{1,0:T(4,128)}, bf16[1,3584,1024]{2,1,0:T(8,128)(2,1)}, bf16[1,1024,3584]{2,1,0:T(8,128)(2,1)}) custom-call(bf16[64,3584]{1,0:T(8,128)(2,1)} %get-tuple-element.9.x, bf16[64,3584]{1,0:T(8,128)(2,1)} %get-tuple-element.10.dyg, bf16[64,1024]{1,0:T(8,128)(2,1)} %get-tuple-element.11.hidden, ...), custom_call_target="tpu_custom_call" | custom-call | flops 939524096 | bytes 14680064 | tf_op jit(solution)/shard_map/pallas_call | solution.py:530
